TPU v7x, 32 devices: a whole 2x2x4 slice. The times are simulated.
32 devices in a mesh: clip: 4 (over y, core), seq: 4 (over z), tp: 2 (over x).
Axes of the slice: x: 2, y: 2, z: 4, core: 2. Of those that a mesh axis runs over, the one named last changes fastest.
Arguments:
- frames: bfloat16 [768, 16, 1152], P('tp', ('clip', 'seq')), parts along dimension 1, may hold values from -6 to 6
- timestep: int32 [4], P('clip'), parts along dimension 0, may hold values from 0 to 999
- embed_weight: bfloat16 [256, 1152], replicated, may hold values from -0.375 to 0.375
- block_weight: bfloat16 [1152, 3456], P(('seq', 'tp')), may hold values from -0.1875 to 0.1875
- spatial_table: float32 [3, 1152], replicated, may hold values from -3 to 3
- temporal_table: float32 [3, 1152], replicated, may hold values from -3 to 3
- spatial_qkv: bfloat16 [1152, 3, 1152], P(None, None, 'tp'), may hold values from -1 to 1
- spatial_out: bfloat16 [1152, 1152], P('tp'), may hold values from -0.1875 to 0.1875
- temporal_qkv: bfloat16 [1152, 3, 1152], P(None, None, 'tp'), may hold values from -1 to 1
- temporal_out: bfloat16 [1152, 1152], P('tp'), may hold values from -0.1875 to 0.1875
Outputs:
- mixed: float32 [768, 16, 1152], P('tp', ('clip', 'seq')), parts along dimension 1
There are 4 independent parts, one for each index of `clip`. A program takes and returns all parts, laid end to end along the dimension named above; an argument that names none is the same for every part. Nothing has to cross between parts.
All inputs are finite; a program needn't handle non-finite values.
Results may differ from a plain program's by a relative error of at most 0.0085.
Values may be sent and summed in bfloat16 or wider, within the bound.
A program may use at most 128 MiB of HBM per device.

v0:
```python
import math

import jax
import jax.numpy as jnp
from jax import lax
from jax.sharding import PartitionSpec as P

HEAD_DIM = 72
FREQ = 256


def layer_norm(values):
    mean = jnp.mean(values, axis=-1, keepdims=True)
    centred = values - mean
    variance = jnp.mean(centred * centred, axis=-1, keepdims=True)
    return centred * lax.rsqrt(variance + 1e-06)


def modulate(tokens, mods):
    normed = layer_norm(tokens.astype(jnp.float32))
    return (normed * (1.0 + mods[1]) + mods[0]).astype(jnp.bfloat16)


def residual_add(tokens, mods, projected):
    return tokens.astype(jnp.float32) + mods[2] * projected


def soft_weights(scores):
    peak = jnp.max(scores, axis=-1, keepdims=True)
    raised = jnp.exp(scores - peak)
    return (raised / jnp.sum(raised, axis=-1, keepdims=True)).astype(jnp.bfloat16)


def time_features(timestep):
    half = FREQ // 2
    ladder = jnp.exp(-math.log(10000.0) * jnp.arange(half, dtype=jnp.float32) / half)
    angles = timestep.astype(jnp.float32)[:, None] * ladder[None, :]
    return jnp.concatenate([jnp.cos(angles), jnp.sin(angles)], axis=-1)


def modulation_rows(timestep, embed_weight, block_weight):
    features = time_features(timestep)
    embedded = jax.nn.silu(
        jnp.dot(features, embed_weight.astype(jnp.float32), precision=lax.Precision.HIGHEST)
    )
    count = block_weight.shape[0]
    start = lax.axis_index(("seq", "tp")) * count
    mine = lax.dynamic_slice_in_dim(embedded, start, count, 1)
    term = jnp.dot(mine, block_weight.astype(jnp.float32), precision=lax.Precision.HIGHEST)
    total = lax.psum(term, ("seq", "tp"))
    return total.reshape(3, -1)


def gather_rows(tokens):
    return lax.all_gather(tokens, "tp", axis=0, tiled=True)


def project_rows(attended, out_weight):
    share = attended.shape[0] // lax.axis_size("tp")

    def term(start, count):
        return jnp.dot(attended, out_weight, preferred_element_type=jnp.float32)

    return lax.psum_scatter(
        term(jnp.int32(0), share * lax.axis_size("tp")), "tp", scatter_dimension=0, tiled=True
    )


def project_in(tokens, qkv_weight):
    flat = qkv_weight.reshape(qkv_weight.shape[0], -1)
    return jnp.dot(tokens, flat, preferred_element_type=jnp.float32).astype(jnp.bfloat16)


def spatial_attend(qkv):
    count, depth = (qkv.shape[0], qkv.shape[1])
    grid = qkv.reshape(count, depth, 3, -1, HEAD_DIM)
    factor = 1.0 / math.sqrt(HEAD_DIM)
    scores = (
        jnp.einsum(
            "qfhd,kfhd->fhqk", grid[:, :, 0], grid[:, :, 1], preferred_element_type=jnp.float32
        )
        * factor
    )
    weights = soft_weights(scores)
    attended = jnp.einsum(
        "fhqk,kfhd->qfhd", weights, grid[:, :, 2], preferred_element_type=jnp.float32
    )
    return attended.astype(jnp.bfloat16).reshape(count, depth, -1)


def temporal_attend(qkv):
    count, depth = (qkv.shape[0], qkv.shape[1])
    grid = qkv.reshape(count, depth, 3, -1, HEAD_DIM)
    factor = 1.0 / math.sqrt(HEAD_DIM)
    scores = (
        jnp.einsum(
            "pfhd,pghd->phfg", grid[:, :, 0], grid[:, :, 1], preferred_element_type=jnp.float32
        )
        * factor
    )
    weights = soft_weights(scores)
    attended = jnp.einsum(
        "phfg,pghd->pfhd", weights, grid[:, :, 2], preferred_element_type=jnp.float32
    )
    return attended.astype(jnp.bfloat16).reshape(count, depth, -1)


def body(
    frames,
    timestep,
    embed_weight,
    block_weight,
    spatial_table,
    temporal_table,
    spatial_qkv,
    spatial_out,
    temporal_qkv,
    temporal_out,
):
    modulation = modulation_rows(timestep, embed_weight, block_weight)
    spatial_mods = spatial_table + modulation
    temporal_mods = temporal_table + modulation
    normed = modulate(frames, spatial_mods)
    whole = gather_rows(normed)
    attended = spatial_attend(project_in(whole, spatial_qkv))
    middle = residual_add(frames, spatial_mods, project_rows(attended, spatial_out))
    normed = modulate(middle, temporal_mods)
    whole = gather_rows(normed)
    qkv = project_in(whole, temporal_qkv)
    moved = lax.all_to_all(qkv, "seq", split_axis=0, concat_axis=1, tiled=True)
    attended = temporal_attend(moved)
    returned = lax.all_to_all(attended, "seq", split_axis=1, concat_axis=0, tiled=True)
    projected = project_rows(returned, temporal_out)
    return residual_add(middle, temporal_mods, projected)


def solution(mesh):
    return jax.shard_map(
        body,
        mesh=mesh,
        in_specs=(
            P("tp", ("clip", "seq"), None),
            P("clip"),
            P(),
            P(("seq", "tp"), None),
            P(),
            P(),
            P(None, None, "tp"),
            P("tp", None),
            P(None, None, "tp"),
            P("tp", None),
        ),
        out_specs=P("tp", ("clip", "seq"), None),
        check_vma=False,
    )
```

profile of v0, /device:TPU:0, one launch (start us, length us, event | category | flops | bytes accessed | tf_op | source)
XLA Modules:
  0.0 412.9 jit_solution(4217502992099497649)
XLA Ops:
  7.4 1.4 convolution_reduce_fusion.1
  8.9 1.7 convolution_reduce_fusion
  10.7 38.8 %psum.7 = f32[3,1152]{1,0:T(4,128)S(1)} all-reduce(f32[3,1152]{1,0:T(4,128)S(1)} %reshape.189), channel_id=1, replica_groups=mesh['clip'=4,'seq'=4,'tp'=2] {'seq','tp'}, use_global_device_ids=true, to_apply=%region_0.1 | all-reduce | flops 3456 | bytes 27648 | tf_op jit(solution)/shard_map/psum | solution.py:50
  52.3 26.8 %all-gather.3.cloned.1.call-done = bf16[768,1,1152]{2,0,1:T(8,128)(2,1)} async-done(((bf16[384,1,1152]{2,0,1:T(8,128)(2,1)}), bf16[768,1,1152]{2,0,1:T(8,128)(2,1)}) %all-gather.3.cloned.1.call-update) | async-done | bytes 1769488 | tf_op jit(solution)/shard_map/all_gather | solution.py:55
  79.1 7.8 %convolution_convert_fusion.1 = bf16[768,1728]{0,1:T(8,128)(2,1)} fusion(bf16[1152,1728]{0,1:T(8,128)(2,1)} %bitcast.88, bf16[768,1,1152]{2,0,1:T(8,128)(2,1)} %all-gather.3.cloned.1.call-done), kind=kOutput, calls=%fused_computation.12 | convolution fusion | flops 3058974720 | bytes 8404992 | tf_op jit(solution)/shard_map/dot_general | solution.py:71
  86.9 10.8 %fusion.43 = (f32[8,768]{1,0:T(8,128)S(1)}, f32[8,768,768]{1,2,0:T(8,128)}) fusion(bf16[768,1,3,8,72]{0,4,3,2,1:T(8,128)(2,1)} %bitcast.90), kind=kOutput, calls=%fused_computation.71 | convolution fusion | flops 693633792 | bytes 20668416 | tf_op jit(solution)/shard_map/sub | solution.py:30
  97.7 8.4 %fusion.29 = bf16[8,72,768]{2,1,0:T(8,128)(2,1)S(1)} fusion(f32[8,768,768]{1,2,0:T(8,128)} %get-tuple-element.17, f32[8,768]{1,0:T(8,128)S(1)} %get-tuple-element.16, bf16[768,1,3,8,72]{0,4,3,2,1:T(8,128)(2,1)} %bitcast.91), kind=kOutput, calls=%fused_computation.39 | convolution fusion | flops 689356800 | bytes 20668416 | tf_op jit(solution)/shard_map/fhqk,kfhd->qfhd/dot_general | solution.py:85
  106.2 3.5 convolution_bitcast_fusion.1
  109.9 47.6 %reduce-scatter.3.cloned.1.call-done = f32[384,1,1152]{2,0,1:T(8,128)} async-done(((f32[768,1,1152]{2,0,1:T(8,128)}), f32[384,1,1152]{2,0,1:T(8,128)}) %reduce-scatter.3.cloned.1.call-update) | async-done | bytes 1769488 | tf_op jit(solution)/shard_map/reduce_scatter | solution.py:64
  157.5 1.9 fusion.40
  161.5 29.5 %all-gather.5.cloned.1.call-done = bf16[768,1,1152]{2,0,1:T(8,128)(2,1)} async-done(((bf16[384,1,1152]{2,0,1:T(8,128)(2,1)}), bf16[768,1,1152]{2,0,1:T(8,128)(2,1)}) %all-gather.5.cloned.1.call-update) | async-done | bytes 1769488 | tf_op jit(solution)/shard_map/all_gather | solution.py:55
  191.0 7.8 %fusion.9 = bf16[768,1,1728]{0,2,1:T(8,128)(2,1)} fusion(bf16[1152,1728]{0,1:T(8,128)(2,1)} %bitcast.89, bf16[768,1,1152]{2,0,1:T(8,128)(2,1)} %all-gather.5.cloned.1.call-done), kind=kOutput, calls=%fused_computation.15 | convolution fusion | flops 3058974720 | bytes 8404992 | tf_op jit(solution)/shard_map/dot_general | solution.py:71
  199.3 5.1 %reduce.24 = bf16[768,1728]{0,1:T(8,128)(2,1)} reduce(bf16[768,1,1728]{0,2,1:T(8,128)(2,1)} %fusion.9, bf16[]{:T(256)} %broadcast.120), dimensions={1}, to_apply=%copy.25.reduce_sub_computation | reduce | bytes 5308418 | tf_op jit(solution)/shard_map/convert_element_type | solution.py:71
  204.4 4.6 %copy.40 = bf16[768,1728]{1,0:T(8,128)(2,1)} copy(bf16[768,1728]{0,1:T(8,128)(2,1)} %reduce.24) | data formatting | bytes 5308416
  209.1 5.8 %reshape.216 = bf16[4,2,165888]{2,1,0:T(2,128)(2,1)} reshape(bf16[768,1728]{1,0:T(8,128)(2,1)} %copy.40) | data formatting | bytes 5308416
  214.8 64.9 %all_to_all.30 = bf16[4,2,165888]{2,1,0:T(2,128)(2,1)} all-to-all(bf16[4,2,165888]{2,1,0:T(2,128)(2,1)} %reshape.216), channel_id=1, replica_groups=mesh['clip'=4,'seq'=4,'tp'=2] {'seq'}, dimensions={0} | all-to-all | bytes 5308416 | tf_op jit(solution)/shard_map/all_to_all | solution.py:130
  279.8 7.1 %reshape.217 = bf16[768,1,1728]{2,1,0:T(2,128)(2,1)} reshape(bf16[4,2,165888]{2,1,0:T(2,128)(2,1)} %all_to_all.30) | data formatting | bytes 5308416
  286.9 4.5 %copy.36 = bf16[768,1,1728]{2,0,1:T(8,128)(2,1)} copy(bf16[768,1,1728]{2,1,0:T(2,128)(2,1)} %reshape.217) | data formatting | bytes 5308416
  291.4 4.7 %copy.26 = bf16[192,4,1,1728]{0,3,1,2:T(8,128)(2,1)} copy(bf16[192,4,1,1728]{3,0,1,2:T(8,128)(2,1)} %bitcast.84) | data formatting | bytes 5308416 | tf_op jit(solution)/shard_map/all_to_all | solution.py:130
  296.2 3.3 fusion.41
  299.4 3.9 copy.38
  303.3 2.2 copy.39
  305.6 3.6 fusion.21
  309.2 4.9 %fusion.44 = (f32[192,8,4]{2,1,0:T(8,128)S(1)}, f32[192,8,4,4]{2,3,1,0:T(4,128)}) fusion(f32[192,8,4,4]{2,3,1,0:T(4,128)S(1)} %fusion.21), kind=kOutput, calls=%fused_computation.72 | output fusion | flops 98307 | bytes 221184 | tf_op jit(solution)/shard_map/sub | solution.py:30
  314.1 2.2 copy.37
  316.4 5.4 %fusion.26 = bf16[192,4,8,72]{3,1,2,0:T(4,128)(2,1)} fusion(f32[192,8,4,4]{2,3,1,0:T(4,128)} %get-tuple-element.19, f32[192,8,4]{2,1,0:T(8,128)S(1)} %get-tuple-element.18, bf16[192,4,1,8,72]{4,1,3,0,2:T(4,128)(2,1)} %copy.37), kind=kOutput, calls=%fused_computation.38 | convolution fusion | flops 4030464 | bytes 1892352 | tf_op jit(solution)/shard_map/phfg,pghd->pfhd/dot_general | solution.py:102
  321.7 2.8 copy.31
  325.2 26.4 %all_to_all.31 = bf16[192,4,576]{2,0,1:T(8,128)(2,1)S(1)} all-to-all(bf16[192,4,576]{2,0,1:T(8,128)(2,1)S(1)} %copy.32), channel_id=1, replica_groups=mesh['clip'=4,'seq'=4,'tp'=2] {'seq'}, dimensions={1} | all-to-all | bytes 1769472 | tf_op jit(solution)/shard_map/all_to_all | solution.py:132
  351.6 3.4 convolution_bitcast_fusion
  355.1 45.9 %reduce-scatter.5.cloned.1.call-done = f32[384,1,1152]{2,0,1:T(8,128)} async-done(((f32[768,1,1152]{2,0,1:T(8,128)}), f32[384,1,1152]{2,0,1:T(8,128)}) %reduce-scatter.5.cloned.1.call-update) | async-done | bytes 1769488 | tf_op jit(solution)/shard_map/reduce_scatter | solution.py:64
  400.9 2.4 multiply_add_fusion
  403.4 3.0 copy.33
  (35 shorter events, 6.4 us)
Async XLA Ops:
  6.5 99.6 %copy-start = (bf16[576,1152]{1,0:T(8,128)(2,1)S(1)}, bf16[576,1152]{1,0:T(8,128)(2,1)}, u32[]{:S(2)}) copy-start(bf16[576,1152]{1,0:T(8,128)(2,1)} %param.17) | copy-start | bytes 3981316
  6.5 43.8 %copy-start.2 = (bf16[384,1,1152]{2,0,1:T(8,128)(2,1)S(1)}, bf16[384,1,1152]{2,0,1:T(8,128)(2,1)}, u32[]{:S(2)}) copy-start(bf16[384,1,1152]{2,0,1:T(8,128)(2,1)} %param.10) | copy-start | bytes 2654212
  6.5 72.6 %all-gather.3.cloned.1.call-start = ((), (), s32[]{:S(2)}) async-start(), calls=%async_computation.4 | async-start | bytes 2654208 | tf_op jit(solution)/shard_map/all_gather | solution.py:55
  52.2 105.3 %reduce-scatter.3.cloned.1.call-start = ((), (), s32[]{:S(2)}) async-start(), calls=%async_computation.5 | async-start | bytes 5308416 | tf_op jit(solution)/shard_map/reduce_scatter | solution.py:64
  109.7 81.3 %all-gather.5.cloned.1.call-start = ((), (), s32[]{:S(2)}) async-start(), calls=%async_computation.6 | async-start | bytes 2654208 | tf_op jit(solution)/shard_map/all_gather | solution.py:55
  157.5 2.0 copy-start.3
  161.4 239.5 %reduce-scatter.5.cloned.1.call-start = ((), (), s32[]{:S(2)}) async-start(), calls=%async_computation.7 | async-start | bytes 5308416 | tf_op jit(solution)/shard_map/reduce_scatter | solution.py:64
  325.2 26.4 %copy-start.4 = (bf16[576,1152]{1,0:T(8,128)(2,1)S(1)}, bf16[576,1152]{1,0:T(8,128)(2,1)}, u32[]{:S(2)}) copy-start(bf16[576,1152]{1,0:T(8,128)(2,1)} %param.19) | copy-start | bytes 3981316
  400.9 5.4 %copy-start.1 = (bf16[576,1152]{1,0:T(8,128)(2,1)S(1)}, bf16[576,1152]{1,0:T(8,128)(2,1)}, u32[]{:S(2)}) copy-start(bf16[576,1152]{1,0:T(8,128)(2,1)} %param.17) | copy-start | bytes 3981316
Sparse Core Ops, SparseCore 0:
  52.4 26.6 all-gather.2
  109.8 47.6 reduce-scatter.2
  161.5 29.4 all-gather.4
  355.2 45.7 reduce-scatter.4
where the time goes:
time: 414 us; the launch traced here: 413 us
  waiting for transfers between devices  150 us (36%)
  blocking collectives  130 us (31%)
  matrix products  54 us (13%)
  local copies, waits for them, and re-layouts  45.5 us (11%)
  other arithmetic  19.1 us (5%)
  between operations  14 us (3%)
    reduce_scatter x2, waiting for transfers between devices, project_rows(): lax.psum_scatter(term(jnp.int32(0), share * lax.axis_size('tp')), 'tp', s...  93.4 us
    all_to_all x1, blocking collectives, body(): moved = lax.all_to_all(qkv, 'seq', split_axis=0, concat_axis=1, tiled=True)  64.9 us
    all_gather x2, waiting for transfers between devices, gather_rows(): return lax.all_gather(tokens, 'tp', axis=0, tiled=True)  56.3 us
    psum x1, blocking collectives, modulation_rows(): total = lax.psum(term, ('seq', 'tp'))  38.8 us
    unnamed x17, local copies, waits for them, and re-layouts  30.6 us
    all_to_all x1, blocking collectives, body(): lax.all_to_all(attended, 'seq', split_axis=1, concat_axis=0, tiled=True)  26.4 us
    dot_general x2, matrix products, project_in(): jnp.dot(tokens, flat, preferred_element_type=jnp.float32)  15.6 us
    sub x1, matrix products, soft_weights(): raised = jnp.exp(scores - peak)  10.8 us
  transfers between devices with their start and end apart: 4, of which 4 were waited for; matrix products, arithmetic and copies ran while one was open for 0% of the time, Pallas kernels for 0%

commit v1 on v0

v1 whole, which is shorter than its diff:
```python
import functools
import math

import jax
import jax.numpy as jnp
from jax import lax
from jax.experimental import pallas as pl
from jax.experimental.pallas import tpu as pltpu
from jax.sharding import PartitionSpec as P

HEAD_DIM = 72
FREQ = 256
F32 = jnp.float32
BF16 = jnp.bfloat16
MESH = pl.DeviceIdType.MESH
NT = (((1,), (1,)), ((), ()))
TN = (((0,), (0,)), ((), ()))
NN = (((1,), (0,)), ((), ()))
FACTOR = 1.0 / math.sqrt(HEAD_DIM)
FACTOR2 = FACTOR * math.log2(math.e)


def time_features(timestep):
    half = FREQ // 2
    ladder = jnp.exp(-math.log(10000.0) * jnp.arange(half, dtype=jnp.float32) / half)
    angles = timestep.astype(jnp.float32)[:, None] * ladder[None, :]
    return jnp.concatenate([jnp.cos(angles), jnp.sin(angles)], axis=-1)


def mm(a, b, dims):
    return lax.dot_general(a, b, dims, preferred_element_type=F32)


def split_rows(row):
    wide = jnp.broadcast_to(row, (8, row.shape[1]))
    first = wide.astype(BF16).astype(F32)
    rest = wide - first
    second = rest.astype(BF16).astype(F32)
    third = rest - second
    index = lax.broadcasted_iota(jnp.int32, wide.shape, 0)
    zero = jnp.zeros_like(wide)
    return jnp.where(
        index == 0, first, jnp.where(index == 1, second, jnp.where(index == 2, third, zero))
    ).astype(BF16)


def normalise(values, scale, shift):
    width = values.shape[1]
    mean = jnp.sum(values, axis=1, keepdims=True) * (1.0 / width)
    centred = values - mean
    variance = jnp.sum(centred * centred, axis=1, keepdims=True) * (1.0 / width)
    return (centred * lax.rsqrt(variance + 1e-06) * (1.0 + scale) + shift).astype(BF16)


def kernel(
    depth,
    feats_ref,
    table_s,
    table_t,
    frames_hbm,
    embed_hbm,
    block_hbm,
    wqs_hbm,
    wos_hbm,
    wqt_hbm,
    wot_hbm,
    out_ref,
    frames,
    embed,
    block,
    wqs,
    wos,
    wqt,
    wot,
    theirs,
    term,
    terms,
    mods_s,
    mods_t,
    qkv,
    att,
    part_send,
    part_recv,
    own,
    middle,
    nt,
    xa,
    xb,
    qkvt,
    attt,
    pb,
    pr,
    po,
    rs,
    rr,
    load_sem,
    term_send,
    term_recv,
    fr_send,
    fr_recv,
    part_ss,
    part_rs,
    nt_send,
    nt_recv,
    fx_send,
    fx_recv,
    pb_send,
    pb_recv,
    rs_send,
    rs_recv,
):
    me_s = lax.axis_index("seq")
    me_t = lax.axis_index("tp")
    peer_t = 1 - me_t
    count, width = frames.shape
    heads = qkv.shape[1]
    pos = nt.shape[1]
    cuts = [(0, 256), (256, count - 256)] if count == 384 else [(0, count)]

    loads = []
    for i, (src, dst) in enumerate(
        [
            (embed_hbm, embed),
            (block_hbm, block),
            (frames_hbm, frames),
            (wqs_hbm, wqs),
            (wos_hbm, wos),
            (wqt_hbm, wqt),
            (wot_hbm, wot),
        ]
    ):
        copy = pltpu.make_async_copy(src, dst, load_sem.at[i])
        copy.start()
        loads.append(copy)

    barrier = pltpu.get_barrier_semaphore()
    peers = [(ds, dt) for ds in range(depth) for dt in range(2) if ds or dt]
    for ds, dt in peers:
        pl.semaphore_signal(
            barrier,
            inc=1,
            device_id={"seq": lax.rem(me_s + ds, depth), "tp": lax.rem(me_t + dt, 2)},
            device_id_type=MESH,
        )
    pl.semaphore_wait(barrier, len(peers))

    frame_copies = []
    for i, (r0, n) in enumerate(cuts):
        copy = pltpu.make_async_remote_copy(
            src_ref=frames_hbm.at[pl.ds(r0, n)],
            dst_ref=theirs.at[pl.ds(r0, n)],
            send_sem=fr_send.at[i],
            recv_sem=fr_recv.at[i],
            device_id={"tp": peer_t},
            device_id_type=MESH,
        )
        copy.start()
        frame_copies.append(copy)

    loads[0].wait()
    hidden = mm(split_rows(feats_ref[...]), embed[...], NN)
    hidden = hidden[0:1] + hidden[1:2] + hidden[2:3]
    hidden = hidden / (1.0 + jnp.exp(-hidden))
    share = block.shape[0]
    start = (me_s * 2 + me_t) * share
    chosen = (
        lax.broadcasted_iota(jnp.int32, (width, share), 0)
        == lax.broadcasted_iota(jnp.int32, (width, share), 1) + start
    )
    mine = mm(split_rows(hidden), chosen.astype(F32).astype(BF16), NN).astype(BF16)
    loads[1].wait()
    spread = mm(mine, block[...], NN)
    spread = spread[0:1] + spread[1:2] + spread[2:3]
    for i in range(3):
        term[i : i + 1, :] = spread[:, i * width : (i + 1) * width]
    term_copies = []
    for i, (ds, dt) in enumerate(peers):
        copy = pltpu.make_async_remote_copy(
            src_ref=term,
            dst_ref=terms.at[i],
            send_sem=term_send.at[i],
            recv_sem=term_recv.at[i],
            device_id={"seq": lax.rem(me_s + ds, depth), "tp": lax.rem(me_t + dt, 2)},
            device_id_type=MESH,
        )
        copy.start()
        term_copies.append(copy)
    total = term[...]
    for i, copy in enumerate(term_copies):
        copy.wait_recv()
        total = total + terms[i]
    mods_s[...] = table_s[...] + total
    mods_t[...] = table_t[...] + total

    def spatial_in(tokens, r0, n, c0):
        normed = jnp.concatenate(
            [
                normalise(
                    tokens[pl.ds(r0 + k, 128), :].astype(F32), mods_s[1:2, :], mods_s[0:1, :]
                )
                for k in range(0, n, 128)
            ],
            axis=0,
        )

        @pl.loop(0, 3)
        def _(j):
            rows = mm(wqs[j], normed, NT)
            qkv[j, :, :, pl.ds(c0, n)] = rows.reshape(heads, HEAD_DIM, n).astype(BF16)

    loads[2].wait()
    loads[3].wait()
    for r0, n in cuts:
        spatial_in(frames, r0, n, r0)
    for i, (r0, n) in enumerate(cuts):
        frame_copies[i].wait_recv()
        spatial_in(theirs, r0, n, count + r0)

    def attend(c0, n):
        @pl.loop(0, heads)
        def _(h):
            scores = mm(qkv[1, h], qkv[0, h, :, pl.ds(c0, n)], TN)
            peak = jnp.max(scores, axis=0, keepdims=True)
            raised = jnp.exp2((scores - peak) * FACTOR2)
            norm = jnp.sum(raised, axis=0, keepdims=True)
            att[h, :, pl.ds(c0, n)] = mm(qkv[2, h], raised.astype(BF16), NN) / norm

    def project(c0, n):
        heads_out = att[:, :, pl.ds(c0, n)].reshape(heads * HEAD_DIM, n).astype(BF16)
        return mm(heads_out, wos[...], TN)

    loads[4].wait()
    part_copies = []
    for i, (r0, n) in enumerate(cuts):
        attend(count + r0, n)
        for k in range(r0, r0 + n, 128):
            part_send[pl.ds(k, 128), :] = project(count + k, 128).astype(BF16)
        copy = pltpu.make_async_remote_copy(
            src_ref=part_send.at[pl.ds(r0, n)],
            dst_ref=part_recv.at[pl.ds(r0, n)],
            send_sem=part_ss.at[i],
            recv_sem=part_rs.at[i],
            device_id={"tp": peer_t},
            device_id_type=MESH,
        )
        copy.start()
        part_copies.append(copy)
    for r0, n in cuts:
        attend(r0, n)
    for k in range(0, count, 128):
        own[pl.ds(k, 128), :] = project(k, 128)

    def seq_copy(src, dst, send, recv, there):
        return pltpu.make_async_remote_copy(
            src_ref=src.at[there],
            dst_ref=dst.at[me_s],
            send_sem=send.at[there],
            recv_sem=recv.at[me_s],
            device_id={"seq": there},
            device_id_type=MESH,
        )

    def seq_arrival(src, dst, send, recv, there):
        return pltpu.make_async_remote_copy(
            src_ref=src.at[there],
            dst_ref=dst.at[there],
            send_sem=send.at[there],
            recv_sem=recv.at[there],
            device_id={"seq": there},
            device_id_type=MESH,
        )

    ready = 0
    for i, (r0, n) in enumerate(cuts):
        part_copies[i].wait_recv()
        for k in range(r0, r0 + n, 128):
            rows = pl.ds(k, 128)
            middle[rows, :] = frames[rows, :].astype(F32) + mods_s[2:3, :] * (
                own[rows, :] + part_recv[rows, :].astype(F32)
            )
        while (ready + 1) * pos <= r0 + n:
            b = ready
            nt[b] = normalise(
                middle[pl.ds(b * pos, pos), :], mods_t[1:2, :], mods_t[0:1, :]
            )

            @pl.when(me_s != b)
            def _():
                seq_copy(nt, xa, nt_send, nt_recv, b).start()

            ready += 1

    def tp_copy(src, dst, send, recv, f):
        return pltpu.make_async_remote_copy(
            src_ref=src.at[f],
            dst_ref=dst.at[f],
            send_sem=send.at[f],
            recv_sem=recv.at[f],
            device_id={"tp": peer_t},
            device_id_type=MESH,
        )

    xa[me_s] = nt[me_s]
    tp_copy(xa, xb, fx_send, fx_recv, me_s).start()
    loads[5].wait()
    loads[6].wait()

    def temporal_in(f):
        tp_copy(xa, xb, fx_send, fx_recv, f).wait_recv()
        if pos % 16:
            both = jnp.concatenate([xa[f].astype(F32), xb[f].astype(F32)], axis=0).astype(BF16)
        else:
            both = jnp.concatenate([xa[f], xb[f]], axis=0)
        for j in range(3):
            rows = mm(wqt[j], both, NT)
            qkvt[j, f] = rows.reshape(heads, HEAD_DIM, 2 * pos).astype(BF16)

    @pl.loop(1, depth)
    def _(d):
        f = lax.rem(me_s + d, depth)
        seq_arrival(nt, xa, nt_send, nt_recv, f).wait_recv()
        tp_copy(xa, xb, fx_send, fx_recv, f).start()
        temporal_in(lax.rem(me_s + d - 1, depth))

    temporal_in(lax.rem(me_s + depth - 1, depth))

    @pl.loop(0, depth)
    def _(d):
        f = lax.rem(me_s + 1 + d, depth)

        @pl.loop(0, heads)
        def _(h):
            query = qkvt[0, f, h].astype(F32)
            scores = [
                jnp.sum(query * qkvt[1, g, h].astype(F32), axis=0, keepdims=True) * FACTOR
                for g in range(depth)
            ]
            peak = functools.reduce(jnp.maximum, scores)
            raised = [jnp.exp(s - peak) for s in scores]
            norm = functools.reduce(jnp.add, raised)
            result = None
            for g in range(depth):
                weight = (raised[g] / norm).astype(BF16).astype(F32)
                piece = weight * qkvt[2, g, h].astype(F32)
                result = piece if result is None else result + piece
            attt[f, h] = result

        flat = attt[f].reshape(heads * HEAD_DIM, 2 * pos).astype(BF16)
        projected = mm(flat, wot[...], TN)
        pb[f] = projected[pos:].astype(BF16)
        tp_copy(pb, pr, pb_send, pb_recv, f).start()
        po[f] = projected[:pos]

    @pl.loop(0, depth)
    def _(d):
        f = lax.rem(me_s + 1 + d, depth)
        tp_copy(pb, pr, pb_send, pb_recv, f).wait_recv()
        rs[f] = (po[f] + pr[f].astype(F32)).astype(BF16)

        @pl.when(d < depth - 1)
        def _():
            seq_copy(rs, rr, rs_send, rs_recv, f).start()

    rr[me_s] = rs[me_s]

    def finish(b):
        rows = pl.ds(pl.multiple_of(b * pos, 8), pos)
        out_ref[rows, :] = middle[rows, :] + mods_t[2:3, :] * rr[b].astype(F32)

    finish(me_s)

    @pl.loop(1, depth)
    def _(d):
        b = lax.rem(me_s + d, depth)
        seq_arrival(rs, rr, rs_send, rs_recv, b).wait_recv()
        finish(b)

    for copy in frame_copies + term_copies + part_copies:
        copy.wait_send()

    @pl.loop(0, depth)
    def _(f):
        tp_copy(xa, xb, fx_send, fx_recv, f).wait_send()
        tp_copy(pb, pr, pb_send, pb_recv, f).wait_send()

        @pl.when(f != me_s)
        def _():
            seq_copy(nt, xa, nt_send, nt_recv, f).wait_send()
            seq_copy(rs, rr, rs_send, rs_recv, f).wait_send()


def body(
    frames,
    timestep,
    embed_weight,
    block_weight,
    spatial_table,
    temporal_table,
    spatial_qkv,
    spatial_out,
    temporal_qkv,
    temporal_out,
):
    depth = lax.axis_size("seq")
    count, _, width = frames.shape
    local = spatial_out.shape[0]
    heads = local // HEAD_DIM
    pos = count // depth
    group = 2 * depth - 1
    vmem = pl.BlockSpec(memory_space=pltpu.VMEM)
    hbm = pl.BlockSpec(memory_space=pl.ANY)
    dma = pltpu.SemaphoreType.DMA
    blocks = pltpu.VMEM((depth, pos, width), BF16)
    result = pl.pallas_call(
        functools.partial(kernel, depth),
        out_shape=jax.ShapeDtypeStruct((count, width), F32),
        in_specs=[vmem] * 3 + [hbm] * 7,
        out_specs=vmem,
        scratch_shapes=[
            pltpu.VMEM((count, width), BF16),
            pltpu.VMEM(embed_weight.shape, BF16),
            pltpu.VMEM(block_weight.shape, BF16),
            pltpu.VMEM((3, local, width), BF16),
            pltpu.VMEM((local, width), BF16),
            pltpu.VMEM((3, local, width), BF16),
            pltpu.VMEM((local, width), BF16),
            pltpu.VMEM((count, width), BF16),
            pltpu.VMEM((3, width), F32),
            pltpu.VMEM((group, 3, width), F32),
            pltpu.VMEM((3, width), F32),
            pltpu.VMEM((3, width), F32),
            pltpu.VMEM((3, heads, HEAD_DIM, 2 * count), BF16),
            pltpu.VMEM((heads, HEAD_DIM, 2 * count), F32),
            pltpu.VMEM((count, width), BF16),
            pltpu.VMEM((count, width), BF16),
            pltpu.VMEM((count, width), F32),
            pltpu.VMEM((count, width), F32),
            blocks,
            blocks,
            blocks,
            pltpu.VMEM((3, depth, heads, HEAD_DIM, 2 * pos), BF16),
            pltpu.VMEM((depth, heads, HEAD_DIM, 2 * pos), F32),
            blocks,
            blocks,
            pltpu.VMEM((depth, pos, width), F32),
            blocks,
            blocks,
            dma((7,)),
            dma((group,)),
            dma((group,)),
            dma((2,)),
            dma((2,)),
            dma((2,)),
            dma((2,)),
            dma((depth,)),
            dma((depth,)),
            dma((depth,)),
            dma((depth,)),
            dma((depth,)),
            dma((depth,)),
            dma((depth,)),
            dma((depth,)),
        ],
        compiler_params=pltpu.CompilerParams(
            collective_id=0, has_side_effects=True, vmem_limit_bytes=58 * 1024 * 1024
        ),
    )(
        time_features(timestep),
        spatial_table,
        temporal_table,
        frames.reshape(count, width),
        embed_weight,
        block_weight,
        jnp.transpose(spatial_qkv, (1, 2, 0)),
        spatial_out,
        jnp.transpose(temporal_qkv, (1, 2, 0)),
        temporal_out,
    )
    return result.reshape(frames.shape)


def solution(mesh):
    return jax.shard_map(
        body,
        mesh=mesh,
        in_specs=(
            P("tp", ("clip", "seq"), None),
            P("clip"),
            P(),
            P(("seq", "tp"), None),
            P(),
            P(),
            P(None, None, "tp"),
            P("tp", None),
            P(None, None, "tp"),
            P("tp", None),
        ),
        out_specs=P("tp", ("clip", "seq"), None),
        check_vma=False,
    )
```

time: 414 us -> 125 us (0.30)
  waiting for transfers between devices: 150 us -> 0 us
  blocking collectives: 130 us -> 0 us
  Pallas kernels: 0 us -> 119 us
  matrix products: 54 us -> 0 us
  local copies, waits for them, and re-layouts: 45.5 us -> 4.5 us
  other arithmetic: 19.1 us -> 0.62 us
  between operations: 14 us -> 0.67 us
    pallas_call x0 -> x1, Pallas kernels: none -> 119 us  [body(): pl.pallas_call(functools.partial(kernel, depth), out_shape=jax.ShapeDtype...]
    reduce_scatter x2 -> x0, waiting for transfers between devices: 93.4 us -> none  [project_rows(): lax.psum_scatter(term(jnp.int32(0), share * lax.axis_size('tp')), 'tp', s...]
    all_to_all x2 -> x0, blocking collectives: 91.4 us -> none  [the longest x1 64.9 us: body(): moved = lax.all_to_all(qkv, 'seq', split_axis=0, concat_axis=1, tiled=True)]
    all_gather x2 -> x0, waiting for transfers between devices: 56.3 us -> none  [gather_rows(): return lax.all_gather(tokens, 'tp', axis=0, tiled=True)]
    dot_general x9 -> x0, matrix products: 43.1 us -> none  [the longest x2 15.6 us: project_in(): jnp.dot(tokens, flat, preferred_element_type=jnp.float32)]
    psum x1 -> x0, blocking collectives: 38.8 us -> none  [modulation_rows(): total = lax.psum(term, ('seq', 'tp'))]
    unnamed x17 -> x0, local copies, waits for them, and re-layouts: 30.6 us -> none
    sub x1 -> x0, matrix products: 10.8 us -> none  [soft_weights(): raised = jnp.exp(scores - peak)]
  transfers between devices with their start and end apart: 4 -> 0, of which waited for: 4 -> 0; matrix products, arithmetic and copies ran while one was open for 0% -> 0% of each run, Pallas kernels for 0% -> 0%
where the time goes in v1:
time: 125 us; the launch traced here: 124 us
  Pallas kernels  119 us (95%)
  local copies, waits for them, and re-layouts  4.5 us (4%)
    pallas_call x1, Pallas kernels, body(): pl.pallas_call(functools.partial(kernel, depth), out_shape=jax.ShapeDtype...  119 us
    reshape x1, local copies, waits for them, and re-layouts, body(): return result.reshape(frames.shape)  4.5 us

profile of v1, /device:TPU:0, one launch (start us, length us, event | category | flops | bytes accessed | tf_op | source)
XLA Modules:
  0.0 124.3 jit_solution(11817939978549278269)
XLA Ops:
  0.7 0.1 fusion
  0.7 0.6 pad_maximum_fusion.feats_ref
  1.3 118.5 %shard_map.100 = f32[384,1152]{1,0:T(8,128)} custom-call(f32[1,256]{1,0:T(1,128)} %pad_maximum_fusion.feats_ref, f32[3,1152]{1,0:T(4,128)} %table_s.1, f32[3,1152]{1,0:T(4,128)} %table_t.1, bf16[384,1152]{1,0:T(8,128)(2,1)} %bitcast.8, bf16[256,1152]{1,0:T(8,128)(2,1)} %embed_hbm.1, bf16[144,3456]{1,0:T(8,128)(2,1)} %block_hbm.1, ...), custom_call_target="tpu_custom_call" | custom-call | tf_op jit(solution)/shard_map/pallas_call | solution.py:414
  119.8 4.5 %copy.11 = f32[384,1,1152]{2,1,0:T(1,128)} copy(f32[384,1,1152]{2,0,1:T(8,128)} %bitcast.5) | data formatting | bytes 3538944 | tf_op jit(solution)/shard_map/reshape | solution.py:479

commit v2 on v1

--- a/solution.py
+++ b/solution.py
@@ -16,6 +16,7 @@
 NT = (((1,), (1,)), ((), ()))
 TN = (((0,), (0,)), ((), ()))
 NN = (((1,), (0,)), ((), ()))
+WAVE_REFS = 20
 FACTOR = 1.0 / math.sqrt(HEAD_DIM)
 FACTOR2 = FACTOR * math.log2(math.e)
 
@@ -54,6 +55,7 @@
 
 def kernel(
     depth,
+    cuts,
     feats_ref,
     table_s,
     table_t,
@@ -64,7 +66,7 @@
     wos_hbm,
     wqt_hbm,
     wot_hbm,
-    out_ref,
+    out_hbm,
     frames,
     embed,
     block,
@@ -83,16 +85,6 @@
     part_recv,
     own,
     middle,
-    nt,
-    xa,
-    xb,
-    qkvt,
-    attt,
-    pb,
-    pr,
-    po,
-    rs,
-    rr,
     load_sem,
     term_send,
     term_recv,
@@ -100,22 +92,14 @@
     fr_recv,
     part_ss,
     part_rs,
-    nt_send,
-    nt_recv,
-    fx_send,
-    fx_recv,
-    pb_send,
-    pb_recv,
-    rs_send,
-    rs_recv,
+    *waves,
 ):
     me_s = lax.axis_index("seq")
     me_t = lax.axis_index("tp")
     peer_t = 1 - me_t
     count, width = frames.shape
     heads = qkv.shape[1]
-    pos = nt.shape[1]
-    cuts = [(0, 256), (256, count - 256)] if count == 384 else [(0, count)]
+    waves = [waves[i * WAVE_REFS : (i + 1) * WAVE_REFS] for i in range(len(cuts))]
 
     loads = []
     for i, (src, dst) in enumerate(
@@ -270,26 +254,6 @@
             device_id_type=MESH,
         )
 
-    ready = 0
-    for i, (r0, n) in enumerate(cuts):
-        part_copies[i].wait_recv()
-        for k in range(r0, r0 + n, 128):
-            rows = pl.ds(k, 128)
-            middle[rows, :] = frames[rows, :].astype(F32) + mods_s[2:3, :] * (
-                own[rows, :] + part_recv[rows, :].astype(F32)
-            )
-        while (ready + 1) * pos <= r0 + n:
-            b = ready
-            nt[b] = normalise(
-                middle[pl.ds(b * pos, pos), :], mods_t[1:2, :], mods_t[0:1, :]
-            )
-
-            @pl.when(me_s != b)
-            def _():
-                seq_copy(nt, xa, nt_send, nt_recv, b).start()
-
-            ready += 1
-
     def tp_copy(src, dst, send, recv, f):
         return pltpu.make_async_remote_copy(
             src_ref=src.at[f],
@@ -300,93 +264,212 @@
             device_id_type=MESH,
         )
 
-    xa[me_s] = nt[me_s]
-    tp_copy(xa, xb, fx_send, fx_recv, me_s).start()
-    loads[5].wait()
-    loads[6].wait()
-
-    def temporal_in(f):
-        tp_copy(xa, xb, fx_send, fx_recv, f).wait_recv()
-        if pos % 16:
-            both = jnp.concatenate([xa[f].astype(F32), xb[f].astype(F32)], axis=0).astype(BF16)
-        else:
-            both = jnp.concatenate([xa[f], xb[f]], axis=0)
-        for j in range(3):
-            rows = mm(wqt[j], both, NT)
-            qkvt[j, f] = rows.reshape(heads, HEAD_DIM, 2 * pos).astype(BF16)
-
-    @pl.loop(1, depth)
-    def _(d):
-        f = lax.rem(me_s + d, depth)
-        seq_arrival(nt, xa, nt_send, nt_recv, f).wait_recv()
-        tp_copy(xa, xb, fx_send, fx_recv, f).start()
-        temporal_in(lax.rem(me_s + d - 1, depth))
-
-    temporal_in(lax.rem(me_s + depth - 1, depth))
-
-    @pl.loop(0, depth)
-    def _(d):
-        f = lax.rem(me_s + 1 + d, depth)
-
-        @pl.loop(0, heads)
-        def _(h):
-            query = qkvt[0, f, h].astype(F32)
-            scores = [
-                jnp.sum(query * qkvt[1, g, h].astype(F32), axis=0, keepdims=True) * FACTOR
-                for g in range(depth)
-            ]
+    def frame_at(d):
+        return lax.rem(me_s + d, depth)
+
+    class Wave:
+        def __init__(self, i):
+            self.i = i
+            self.r0, self.n = cuts[i]
+            self.pos = self.n // depth
+            (
+                self.nt,
+                self.xa,
+                self.xb,
+                self.qkvt,
+                self.attt,
+                self.pb,
+                self.pr,
+                self.po,
+                self.rs,
+                self.rr,
+                self.nt_send,
+                self.nt_recv,
+                self.fx_send,
+                self.fx_recv,
+                self.pb_send,
+                self.pb_recv,
+                self.rs_send,
+                self.rs_recv,
+                self.out_sem,
+                self.outbuf,
+            ) = waves[i]
+
+        def middle_out(self):
+            part_copies[self.i].wait_recv()
+            for k in range(self.r0, self.r0 + self.n, 128):
+                rows = pl.ds(k, 128)
+                middle[rows, :] = frames[rows, :].astype(F32) + mods_s[2:3, :] * (
+                    own[rows, :] + part_recv[rows, :].astype(F32)
+                )
+
+            @pl.loop(1, depth + 1)
+            def _(d):
+                b = frame_at(d)
+                rows = pl.ds(pl.multiple_of(self.r0 + b * self.pos, 8), self.pos)
+                self.nt[b] = normalise(middle[rows, :], mods_t[1:2, :], mods_t[0:1, :])
+
+                @pl.when(d < depth)
+                def _():
+                    seq_copy(self.nt, self.xa, self.nt_send, self.nt_recv, b).start()
+
+            self.xa[me_s] = self.nt[me_s]
+            tp_copy(self.xa, self.xb, self.fx_send, self.fx_recv, me_s).start()
+
+        def forward(self, d):
+            f = frame_at(d)
+            seq_arrival(self.nt, self.xa, self.nt_send, self.nt_recv, f).wait_recv()
+            tp_copy(self.xa, self.xb, self.fx_send, self.fx_recv, f).start()
+
+        def batches(self):
+            size = min(depth, max(1, 256 // (2 * self.pos)))
+            return [range(d, min(d + size, depth)) for d in range(0, depth, size)]
+
+        def project_in(self, batch):
+            parts = []
+            for d in batch:
+                f = frame_at(d)
+                tp_copy(self.xa, self.xb, self.fx_send, self.fx_recv, f).wait_recv()
+                parts += [self.xa[f], self.xb[f]]
+            if self.pos % 16:
+                parts = [part.astype(F32) for part in parts]
+            tokens = jnp.concatenate(parts, axis=0).astype(BF16)
+            span = 2 * self.pos
+            for j in range(3):
+                rows = mm(wqt[j], tokens, NT).reshape(heads, HEAD_DIM, -1)
+                for k, d in enumerate(batch):
+                    self.qkvt[j, frame_at(d)] = rows[:, :, k * span : (k + 1) * span].astype(BF16)
+
+        def attend(self, d):
+            f = frame_at(d)
+            scores = []
+            for g in range(depth):
+                scores.append([])
+            for h in range(heads):
+                query = self.qkvt[0, f, h].astype(F32)
+                for g in range(depth):
+                    key = self.qkvt[1, g, h].astype(F32)
+                    scores[g].append(jnp.sum(query * key, axis=0, keepdims=True))
+            scores = [jnp.concatenate(rows, axis=0) * FACTOR for rows in scores]
             peak = functools.reduce(jnp.maximum, scores)
             raised = [jnp.exp(s - peak) for s in scores]
             norm = functools.reduce(jnp.add, raised)
-            result = None
-            for g in range(depth):
-                weight = (raised[g] / norm).astype(BF16).astype(F32)
-                piece = weight * qkvt[2, g, h].astype(F32)
-                result = piece if result is None else result + piece
-            attt[f, h] = result
-
-        flat = attt[f].reshape(heads * HEAD_DIM, 2 * pos).astype(BF16)
-        projected = mm(flat, wot[...], TN)
-        pb[f] = projected[pos:].astype(BF16)
-        tp_copy(pb, pr, pb_send, pb_recv, f).start()
-        po[f] = projected[:pos]
+            weights = [(r / norm).astype(BF16).astype(F32) for r in raised]
+            for h in range(heads):
+                result = None
+                for g in range(depth):
+                    piece = weights[g][h : h + 1, :] * self.qkvt[2, g, h].astype(F32)
+                    result = piece if result is None else result + piece
+                self.attt[h] = result
+            flat = self.attt[...].reshape(heads * HEAD_DIM, 2 * self.pos).astype(BF16)
+            projected = mm(flat, wot[...], TN)
+            self.pb[f] = projected[self.pos :].astype(BF16)
+            tp_copy(self.pb, self.pr, self.pb_send, self.pb_recv, f).start()
+            self.po[f] = projected[: self.pos]
+
+        def send_back(self, d):
+            f = frame_at(d)
+            tp_copy(self.pb, self.pr, self.pb_send, self.pb_recv, f).wait_recv()
+            self.rs[f] = (self.po[f] + self.pr[f].astype(F32)).astype(BF16)
+
+            @pl.when(f != me_s)
+            def _():
+                seq_copy(self.rs, self.rr, self.rs_send, self.rs_recv, f).start()
+
+        def out_copy(self, b):
+            return pltpu.make_async_copy(
+                self.outbuf.at[b],
+                out_hbm.at[pl.ds(self.r0 + b * self.pos, self.pos), 0, :],
+                self.out_sem.at[b],
+            )
+
+        def finish(self, b, back):
+            rows = pl.ds(pl.multiple_of(self.r0 + b * self.pos, 8), self.pos)
+            self.outbuf[b] = middle[rows, :] + mods_t[2:3, :] * back[b].astype(F32)
+            self.out_copy(b).start()
+
+        def finish_all(self):
+            self.finish(me_s, self.rs)
+
+            @pl.loop(1, depth)
+            def _(d):
+                b = frame_at(d)
+                seq_arrival(self.rs, self.rr, self.rs_send, self.rs_recv, b).wait_recv()
+                self.finish(b, self.rr)
+
+        def drain(self):
+            @pl.loop(0, depth)
+            def _(f):
+                tp_copy(self.xa, self.xb, self.fx_send, self.fx_recv, f).wait_send()
+                tp_copy(self.pb, self.pr, self.pb_send, self.pb_recv, f).wait_send()
+                self.out_copy(f).wait()
+
+                @pl.when(f != me_s)
+                def _():
+                    seq_copy(self.nt, self.xa, self.nt_send, self.nt_recv, f).wait_send()
+                    seq_copy(self.rs, self.rr, self.rs_send, self.rs_recv, f).wait_send()
+
+    steps = [Wave(i) for i in range(len(cuts))]
+    for wave in steps:
+        wave.middle_out()
+    loads[5].wait()
+    loads[6].wait()
+
+    before = None
+    for wave in steps:
+        for batch in wave.batches():
+            for d in batch:
+                if d:
+                    wave.forward(d)
+            if before is not None:
+                for d in batch:
+                    before.send_back((d + 1) % depth)
+            wave.project_in(batch)
+
+        @pl.loop(0, depth)
+        def _(d):
+            wave.attend(d + 1)
+
+        before = wave
 
     @pl.loop(0, depth)
     def _(d):
-        f = lax.rem(me_s + 1 + d, depth)
-        tp_copy(pb, pr, pb_send, pb_recv, f).wait_recv()
-        rs[f] = (po[f] + pr[f].astype(F32)).astype(BF16)
-
-        @pl.when(d < depth - 1)
-        def _():
-            seq_copy(rs, rr, rs_send, rs_recv, f).start()
-
-    rr[me_s] = rs[me_s]
-
-    def finish(b):
-        rows = pl.ds(pl.multiple_of(b * pos, 8), pos)
-        out_ref[rows, :] = middle[rows, :] + mods_t[2:3, :] * rr[b].astype(F32)
-
-    finish(me_s)
-
-    @pl.loop(1, depth)
-    def _(d):
-        b = lax.rem(me_s + d, depth)
-        seq_arrival(rs, rr, rs_send, rs_recv, b).wait_recv()
-        finish(b)
+        before.send_back(d + 1)
+
+    for wave in steps:
+        wave.finish_all()
 
     for copy in frame_copies + term_copies + part_copies:
         copy.wait_send()
-
-    @pl.loop(0, depth)
-    def _(f):
-        tp_copy(xa, xb, fx_send, fx_recv, f).wait_send()
-        tp_copy(pb, pr, pb_send, pb_recv, f).wait_send()
-
-        @pl.when(f != me_s)
-        def _():
-            seq_copy(nt, xa, nt_send, nt_recv, f).wait_send()
-            seq_copy(rs, rr, rs_send, rs_recv, f).wait_send()
+    for wave in steps:
+        wave.drain()
+
+
+def wave_scratch(depth, pos, width, heads):
+    dma = pltpu.SemaphoreType.DMA
+    blocks = pltpu.VMEM((depth, pos, width), BF16)
+    return [
+        blocks,
+        blocks,
+        blocks,
+        pltpu.VMEM((3, depth, heads, HEAD_DIM, 2 * pos), BF16),
+        pltpu.VMEM((heads, HEAD_DIM, 2 * pos), F32),
+        blocks,
+        blocks,
+        pltpu.VMEM((depth, pos, width), F32),
+        blocks,
+        blocks,
+        dma((depth,)),
+        dma((depth,)),
+        dma((depth,)),
+        dma((depth,)),
+        dma((depth,)),
+        dma((depth,)),
+        dma((depth,)),
+        dma((depth,)),
+        dma((depth,)),
+        pltpu.VMEM((depth, pos, width), F32),
+    ]
 
 
 def body(
@@ -405,17 +488,19 @@
     count, _, width = frames.shape
     local = spatial_out.shape[0]
     heads = local // HEAD_DIM
-    pos = count // depth
+    cuts = [(0, 256), (256, count - 256)] if count == 384 else [(0, count)]
+    waves = []
+    for _, rows in cuts:
+        waves += wave_scratch(depth, rows // depth, width, heads)
     group = 2 * depth - 1
     vmem = pl.BlockSpec(memory_space=pltpu.VMEM)
     hbm = pl.BlockSpec(memory_space=pl.ANY)
     dma = pltpu.SemaphoreType.DMA
-    blocks = pltpu.VMEM((depth, pos, width), BF16)
     result = pl.pallas_call(
-        functools.partial(kernel, depth),
-        out_shape=jax.ShapeDtypeStruct((count, width), F32),
+        functools.partial(kernel, depth, cuts),
+        out_shape=jax.ShapeDtypeStruct((count, 1, width), F32),
         in_specs=[vmem] * 3 + [hbm] * 7,
-        out_specs=vmem,
+        out_specs=hbm,
         scratch_shapes=[
             pltpu.VMEM((count, width), BF16),
             pltpu.VMEM(embed_weight.shape, BF16),
@@ -435,16 +520,6 @@
             pltpu.VMEM((count, width), BF16),
             pltpu.VMEM((count, width), F32),
             pltpu.VMEM((count, width), F32),
-            blocks,
-            blocks,
-            blocks,
-            pltpu.VMEM((3, depth, heads, HEAD_DIM, 2 * pos), BF16),
-            pltpu.VMEM((depth, heads, HEAD_DIM, 2 * pos), F32),
-            blocks,
-            blocks,
-            pltpu.VMEM((depth, pos, width), F32),
-            blocks,
-            blocks,
             dma((7,)),
             dma((group,)),
             dma((group,)),
@@ -452,15 +527,8 @@
             dma((2,)),
             dma((2,)),
             dma((2,)),
-            dma((depth,)),
-            dma((depth,)),
-            dma((depth,)),
-            dma((depth,)),
-            dma((depth,)),
-            dma((depth,)),
-            dma((depth,)),
-            dma((depth,)),
-        ],
+        ]
+        + waves,
         compiler_params=pltpu.CompilerParams(
             collective_id=0, has_side_effects=True, vmem_limit_bytes=58 * 1024 * 1024
         ),
@@ -476,7 +544,7 @@
         jnp.transpose(temporal_qkv, (1, 2, 0)),
         temporal_out,
     )
-    return result.reshape(frames.shape)
+    return result
 
 
 def solution(mesh):

time: 125 us -> 126 us (level)
    reshape x1 -> x0, local copies, waits for them, and re-layouts: 4.5 us -> none  [body(): return result.reshape(frames.shape)]
    unnamed x0 -> x1, local copies, waits for them, and re-layouts: none -> 3.9 us
    pallas_call x1, Pallas kernels: 119 us -> 120 us  [body(): pl.pallas_call(functools.partial(kernel, depth, cuts), out_shape=jax.Shap...]
where the time goes in v2:
time: 126 us; the launch traced here: 125 us
  Pallas kernels  120 us (95%)
  local copies, waits for them, and re-layouts  3.9 us (3%)
    pallas_call x1, Pallas kernels, body(): pl.pallas_call(functools.partial(kernel, depth, cuts), out_shape=jax.Shap...  120 us
    unnamed x1, local copies, waits for them, and re-layouts  3.9 us

profile of v2, /device:TPU:0, one launch (start us, length us, event | category | flops | bytes accessed | tf_op | source)
XLA Modules:
  0.0 125.5 jit_solution(9530417405250662809)
XLA Ops:
  0.7 0.1 fusion
  0.7 0.6 pad_maximum_fusion.feats_ref
  1.3 120.3 %shard_map.100 = f32[384,1,1152]{2,1,0:T(1,128)} custom-call(f32[1,256]{1,0:T(1,128)} %pad_maximum_fusion.feats_ref, f32[3,1152]{1,0:T(4,128)} %table_s.1, f32[3,1152]{1,0:T(4,128)} %table_t.1, bf16[384,1152]{1,0:T(8,128)(2,1)} %bitcast.6, bf16[256,1152]{1,0:T(8,128)(2,1)} %embed_hbm.1, bf16[144,3456]{1,0:T(8,128)(2,1)} %block_hbm.1, ...), custom_call_target="tpu_custom_call" | custom-call | tf_op jit(solution)/shard_map/pallas_call | solution.py:499
  121.6 3.9 %copy.13 = f32[384,1,1152]{2,1,0:T(1,128)} copy(f32[384,1,1152]{2,1,0:T(1,128)} %shard_map.100) | data formatting | bytes 3538944

commit v3 on v2

--- a/solution.py
+++ b/solution.py
@@ -16,7 +16,7 @@
 NT = (((1,), (1,)), ((), ()))
 TN = (((0,), (0,)), ((), ()))
 NN = (((1,), (0,)), ((), ()))
-WAVE_REFS = 20
+WAVE_REFS = 18
 FACTOR = 1.0 / math.sqrt(HEAD_DIM)
 FACTOR2 = FACTOR * math.log2(math.e)
 
@@ -66,7 +66,7 @@
     wos_hbm,
     wqt_hbm,
     wot_hbm,
-    out_hbm,
+    out_ref,
     frames,
     embed,
     block,
@@ -92,6 +92,10 @@
     fr_recv,
     part_ss,
     part_rs,
+    keys,
+    wot_other,
+    wx_send,
+    wx_recv,
     *waves,
 ):
     me_s = lax.axis_index("seq")
@@ -126,7 +130,17 @@
             device_id={"seq": lax.rem(me_s + ds, depth), "tp": lax.rem(me_t + dt, 2)},
             device_id_type=MESH,
         )
-    pl.semaphore_wait(barrier, len(peers))
+    parts = wx_send.shape[0]
+    me_c = lax.axis_index("clip")
+    piece = lax.rem(me_c, parts)
+    for k in range(1, parts):
+        pl.semaphore_signal(
+            barrier,
+            inc=1,
+            device_id={"clip": me_c - piece + lax.rem(piece + k, parts)},
+            device_id_type=MESH,
+        )
+    pl.semaphore_wait(barrier, len(peers) + parts - 1)
 
     frame_copies = []
     for i, (r0, n) in enumerate(cuts):
@@ -189,8 +203,13 @@
 
         @pl.loop(0, 3)
         def _(j):
-            rows = mm(wqs[j], normed, NT)
-            qkv[j, :, :, pl.ds(c0, n)] = rows.reshape(heads, HEAD_DIM, n).astype(BF16)
+            rows = mm(wqs[j], normed, NT).reshape(heads, HEAD_DIM, n)
+            qkv[j, :, :, pl.ds(c0, n)] = rows.astype(BF16)
+
+            @pl.when(j == 1)
+            def _():
+                for h in range(heads):
+                    keys[h, pl.ds(c0, n), :] = rows[h].T.astype(BF16)
 
     loads[2].wait()
     loads[3].wait()
@@ -198,12 +217,24 @@
         spatial_in(frames, r0, n, r0)
     for i, (r0, n) in enumerate(cuts):
         frame_copies[i].wait_recv()
+        if i == len(cuts) - 1:
+            slice_rows = wot.shape[0] // parts
+            wot_rows = pl.ds(pl.multiple_of(piece * slice_rows, 16), slice_rows)
+            wot_fetch = pltpu.make_async_remote_copy(
+                src_ref=wot_hbm.at[wot_rows],
+                dst_ref=wot_other.at[wot_rows],
+                send_sem=wx_send.at[0],
+                recv_sem=wx_recv.at[0],
+                device_id={"tp": peer_t},
+                device_id_type=MESH,
+            )
+            wot_fetch.start()
         spatial_in(theirs, r0, n, count + r0)
 
     def attend(c0, n):
         @pl.loop(0, heads)
         def _(h):
-            scores = mm(qkv[1, h], qkv[0, h, :, pl.ds(c0, n)], TN)
+            scores = mm(keys[h], qkv[0, h, :, pl.ds(c0, n)], NN)
             peak = jnp.max(scores, axis=0, keepdims=True)
             raised = jnp.exp2((scores - peak) * FACTOR2)
             norm = jnp.sum(raised, axis=0, keepdims=True)
@@ -229,6 +260,19 @@
         )
         copy.start()
         part_copies.append(copy)
+    wot_fetch.wait_recv()
+    wot_copies = []
+    for k in range(1, parts):
+        copy = pltpu.make_async_remote_copy(
+            src_ref=wot_other.at[wot_rows],
+            dst_ref=wot_other.at[wot_rows],
+            send_sem=wx_send.at[k],
+            recv_sem=wx_recv.at[k],
+            device_id={"clip": me_c - piece + lax.rem(piece + k, parts)},
+            device_id_type=MESH,
+        )
+        copy.start()
+        wot_copies.append(copy)
     for r0, n in cuts:
         attend(r0, n)
     for k in range(0, count, 128):
@@ -291,8 +335,6 @@
                 self.pb_recv,
                 self.rs_send,
                 self.rs_recv,
-                self.out_sem,
-                self.outbuf,
             ) = waves[i]
 
         def middle_out(self):
@@ -361,32 +403,25 @@
                     piece = weights[g][h : h + 1, :] * self.qkvt[2, g, h].astype(F32)
                     result = piece if result is None else result + piece
                 self.attt[h] = result
-            flat = self.attt[...].reshape(heads * HEAD_DIM, 2 * self.pos).astype(BF16)
-            projected = mm(flat, wot[...], TN)
-            self.pb[f] = projected[self.pos :].astype(BF16)
+            flat = self.attt[...].reshape(heads * HEAD_DIM, 2 * self.pos).T
+            self.pb[f] = flat[self.pos :].astype(BF16)
             tp_copy(self.pb, self.pr, self.pb_send, self.pb_recv, f).start()
-            self.po[f] = projected[: self.pos]
+            self.po[f] = flat[: self.pos].astype(BF16)
 
         def send_back(self, d):
             f = frame_at(d)
             tp_copy(self.pb, self.pr, self.pb_send, self.pb_recv, f).wait_recv()
-            self.rs[f] = (self.po[f] + self.pr[f].astype(F32)).astype(BF16)
+            self.rs[f] = (
+                mm(self.po[f], wot[...], NN) + mm(self.pr[f], wot_other[...], NN)
+            ).astype(BF16)
 
             @pl.when(f != me_s)
             def _():
                 seq_copy(self.rs, self.rr, self.rs_send, self.rs_recv, f).start()
 
-        def out_copy(self, b):
-            return pltpu.make_async_copy(
-                self.outbuf.at[b],
-                out_hbm.at[pl.ds(self.r0 + b * self.pos, self.pos), 0, :],
-                self.out_sem.at[b],
-            )
-
         def finish(self, b, back):
             rows = pl.ds(pl.multiple_of(self.r0 + b * self.pos, 8), self.pos)
-            self.outbuf[b] = middle[rows, :] + mods_t[2:3, :] * back[b].astype(F32)
-            self.out_copy(b).start()
+            out_ref[rows, :] = middle[rows, :] + mods_t[2:3, :] * back[b].astype(F32)
 
         def finish_all(self):
             self.finish(me_s, self.rs)
@@ -402,7 +437,6 @@
             def _(f):
                 tp_copy(self.xa, self.xb, self.fx_send, self.fx_recv, f).wait_send()
                 tp_copy(self.pb, self.pr, self.pb_send, self.pb_recv, f).wait_send()
-                self.out_copy(f).wait()
 
                 @pl.when(f != me_s)
                 def _():
@@ -422,6 +456,9 @@
                 if d:
                     wave.forward(d)
             if before is not None:
+                if batch[0] == 0:
+                    for copy in wot_copies:
+                        copy.wait_recv()
                 for d in batch:
                     before.send_back((d + 1) % depth)
             wave.project_in(batch)
@@ -432,6 +469,10 @@
 
         before = wave
 
+    if len(steps) == 1:
+        for copy in wot_copies:
+            copy.wait_recv()
+
     @pl.loop(0, depth)
     def _(d):
         before.send_back(d + 1)
@@ -439,7 +480,7 @@
     for wave in steps:
         wave.finish_all()
 
-    for copy in frame_copies + term_copies + part_copies:
+    for copy in frame_copies + term_copies + part_copies + [wot_fetch] + wot_copies:
         copy.wait_send()
     for wave in steps:
         wave.drain()
@@ -448,28 +489,41 @@
 def wave_scratch(depth, pos, width, heads):
     dma = pltpu.SemaphoreType.DMA
     blocks = pltpu.VMEM((depth, pos, width), BF16)
+    halves = pltpu.VMEM((depth, pos, heads * HEAD_DIM), BF16)
     return [
         blocks,
         blocks,
         blocks,
         pltpu.VMEM((3, depth, heads, HEAD_DIM, 2 * pos), BF16),
         pltpu.VMEM((heads, HEAD_DIM, 2 * pos), F32),
+        halves,
+        halves,
+        halves,
         blocks,
         blocks,
-        pltpu.VMEM((depth, pos, width), F32),
-        blocks,
-        blocks,
-        dma((depth,)),
-        dma((depth,)),
-        dma((depth,)),
-        dma((depth,)),
-        dma((depth,)),
-        dma((depth,)),
-        dma((depth,)),
-        dma((depth,)),
-        dma((depth,)),
-        pltpu.VMEM((depth, pos, width), F32),
+        dma((depth,)),
+        dma((depth,)),
+        dma((depth,)),
+        dma((depth,)),
+        dma((depth,)),
+        dma((depth,)),
+        dma((depth,)),
+        dma((depth,)),
     ]
+
+
+def write_out(src, dst, sem):
+    rows = src.shape[0] // 3
+    copies = [
+        pltpu.make_async_copy(
+            src.at[pl.ds(i * rows, rows)], dst.at[pl.ds(i * rows, rows), 0, :], sem.at[i]
+        )
+        for i in range(3)
+    ]
+    for copy in copies:
+        copy.start()
+    for copy in copies:
+        copy.wait()
 
 
 def body(
@@ -489,6 +543,7 @@
     local = spatial_out.shape[0]
     heads = local // HEAD_DIM
     cuts = [(0, 256), (256, count - 256)] if count == 384 else [(0, count)]
+    parts = min(4, lax.axis_size("clip"))
     waves = []
     for _, rows in cuts:
         waves += wave_scratch(depth, rows // depth, width, heads)
@@ -498,9 +553,9 @@
     dma = pltpu.SemaphoreType.DMA
     result = pl.pallas_call(
         functools.partial(kernel, depth, cuts),
-        out_shape=jax.ShapeDtypeStruct((count, 1, width), F32),
+        out_shape=jax.ShapeDtypeStruct((count, width), F32),
         in_specs=[vmem] * 3 + [hbm] * 7,
-        out_specs=hbm,
+        out_specs=vmem,
         scratch_shapes=[
             pltpu.VMEM((count, width), BF16),
             pltpu.VMEM(embed_weight.shape, BF16),
@@ -527,6 +582,10 @@
             dma((2,)),
             dma((2,)),
             dma((2,)),
+            pltpu.VMEM((heads, 2 * count, HEAD_DIM), BF16),
+            pltpu.VMEM((local, width), BF16),
+            dma((parts,)),
+            dma((parts,)),
         ]
         + waves,
         compiler_params=pltpu.CompilerParams(
@@ -544,7 +603,13 @@
         jnp.transpose(temporal_qkv, (1, 2, 0)),
         temporal_out,
     )
-    return result
+    return pl.pallas_call(
+        write_out,
+        out_shape=jax.ShapeDtypeStruct(frames.shape, F32),
+        in_specs=[hbm],
+        out_specs=hbm,
+        scratch_shapes=[dma((3,))],
+    )(result)
 
 
 def solution(mesh):

time: 126 us -> 167 us (1.33)
  Pallas kernels: 120 us -> 165 us
  local copies, waits for them, and re-layouts: 3.9 us -> 0 us
    pallas_call x0 -> x1, Pallas kernels: none -> 54.7 us  [body(): pl.pallas_call(write_out, out_shape=jax.ShapeDtypeStruct(frames.shape, F3...]
    pallas_call x1, Pallas kernels: 120 us -> 111 us  [body(): pl.pallas_call(functools.partial(kernel, depth, cuts), out_shape=jax.Shap...]
    unnamed x1 -> x0, local copies, waits for them, and re-layouts: 3.9 us -> none
where the time goes in v3:
time: 167 us
  Pallas kernels  165 us (99%)
    pallas_call x1, Pallas kernels, body(): pl.pallas_call(functools.partial(kernel, depth, cuts), out_shape=jax.Shap...  111 us
    pallas_call x1, Pallas kernels, body(): pl.pallas_call(write_out, out_shape=jax.ShapeDtypeStruct(frames.shape, F3...  54.7 us

profile of v3, /device:TPU:0, one launch (start us, length us, event | category | flops | bytes accessed | tf_op | source)
XLA Modules:
  0.0 166.6 jit_solution(16550522036855247950)
XLA Ops:
  0.7 0.1 fusion
  0.7 0.6 pad_maximum_fusion.feats_ref
  1.3 110.6 %shard_map.100.src = f32[384,1152]{1,0:T(8,128)} custom-call(f32[1,256]{1,0:T(1,128)} %pad_maximum_fusion.feats_ref, f32[3,1152]{1,0:T(4,128)} %table_s.1, f32[3,1152]{1,0:T(4,128)} %table_t.1, bf16[384,1152]{1,0:T(8,128)(2,1)} %bitcast.6, bf16[256,1152]{1,0:T(8,128)(2,1)} %embed_hbm.1, bf16[144,3456]{1,0:T(8,128)(2,1)} %block_hbm.1, ...), custom_call_target="tpu_custom_call" | custom-call | tf_op jit(solution)/shard_map/pallas_call | solution.py:554
  111.9 54.7 %shard_map.101 = f32[384,1,1152]{2,1,0:T(1,128)} custom-call(f32[384,1152]{1,0:T(8,128)} %shard_map.100.src), custom_call_target="tpu_custom_call" | custom-call | tf_op jit(solution)/shard_map/pallas_call | solution.py:606

commit v4 on v3

--- a/solution.py
+++ b/solution.py
@@ -96,6 +96,8 @@
     wot_other,
     wx_send,
     wx_recv,
+    peaks,
+    norms,
     *waves,
 ):
     me_s = lax.axis_index("seq")
@@ -211,10 +213,36 @@
                 for h in range(heads):
                     keys[h, pl.ds(c0, n), :] = rows[h].T.astype(BF16)
 
+    def attend(c0, n, k0, extent, first, last):
+        here = pl.ds(c0, n)
+
+        @pl.loop(0, heads)
+        def _(h):
+            scores = mm(keys[h, pl.ds(k0, extent), :], qkv[0, h, :, here], NN)
+            peak = jnp.max(scores, axis=0, keepdims=True)
+            if not first:
+                before = peaks[h, :, here]
+                peak = jnp.maximum(peak, before)
+                shrink = jnp.exp2((before - peak) * FACTOR2)
+            raised = jnp.exp2((scores - peak) * FACTOR2)
+            norm = jnp.sum(raised, axis=0, keepdims=True)
+            result = mm(qkv[2, h, :, pl.ds(k0, extent)], raised.astype(BF16), NN)
+            if not first:
+                norm = norm + norms[h, :, here] * shrink
+                result = result + att[h, :, here] * shrink
+            if last:
+                att[h, :, here] = result / norm
+            else:
+                peaks[h, :, here] = peak
+                norms[h, :, here] = norm
+                att[h, :, here] = result
+
     loads[2].wait()
     loads[3].wait()
     for r0, n in cuts:
         spatial_in(frames, r0, n, r0)
+    for r0, n in cuts:
+        attend(r0, n, 0, count, True, False)
     for i, (r0, n) in enumerate(cuts):
         frame_copies[i].wait_recv()
         if i == len(cuts) - 1:
@@ -230,15 +258,8 @@
             )
             wot_fetch.start()
         spatial_in(theirs, r0, n, count + r0)
-
-    def attend(c0, n):
-        @pl.loop(0, heads)
-        def _(h):
-            scores = mm(keys[h], qkv[0, h, :, pl.ds(c0, n)], NN)
-            peak = jnp.max(scores, axis=0, keepdims=True)
-            raised = jnp.exp2((scores - peak) * FACTOR2)
-            norm = jnp.sum(raised, axis=0, keepdims=True)
-            att[h, :, pl.ds(c0, n)] = mm(qkv[2, h], raised.astype(BF16), NN) / norm
+        if i < len(cuts) - 1:
+            attend(count + r0, n, 0, count + r0 + n, True, False)
 
     def project(c0, n):
         heads_out = att[:, :, pl.ds(c0, n)].reshape(heads * HEAD_DIM, n).astype(BF16)
@@ -247,7 +268,10 @@
     loads[4].wait()
     part_copies = []
     for i, (r0, n) in enumerate(cuts):
-        attend(count + r0, n)
+        if i < len(cuts) - 1:
+            attend(count + r0, n, count + r0 + n, count - r0 - n, False, True)
+        else:
+            attend(count + r0, n, 0, 2 * count, True, True)
         for k in range(r0, r0 + n, 128):
             part_send[pl.ds(k, 128), :] = project(count + k, 128).astype(BF16)
         copy = pltpu.make_async_remote_copy(
@@ -274,7 +298,7 @@
         copy.start()
         wot_copies.append(copy)
     for r0, n in cuts:
-        attend(r0, n)
+        attend(r0, n, count, count, False, True)
     for k in range(0, count, 128):
         own[pl.ds(k, 128), :] = project(k, 128)
 
@@ -510,20 +534,6 @@
         dma((depth,)),
         dma((depth,)),
     ]
-
-
-def write_out(src, dst, sem):
-    rows = src.shape[0] // 3
-    copies = [
-        pltpu.make_async_copy(
-            src.at[pl.ds(i * rows, rows)], dst.at[pl.ds(i * rows, rows), 0, :], sem.at[i]
-        )
-        for i in range(3)
-    ]
-    for copy in copies:
-        copy.start()
-    for copy in copies:
-        copy.wait()
 
 
 def body(
@@ -586,6 +596,8 @@
             pltpu.VMEM((local, width), BF16),
             dma((parts,)),
             dma((parts,)),
+            pltpu.VMEM((heads, 1, 2 * count), F32),
+            pltpu.VMEM((heads, 1, 2 * count), F32),
         ]
         + waves,
         compiler_params=pltpu.CompilerParams(
@@ -603,13 +615,7 @@
         jnp.transpose(temporal_qkv, (1, 2, 0)),
         temporal_out,
     )
-    return pl.pallas_call(
-        write_out,
-        out_shape=jax.ShapeDtypeStruct(frames.shape, F32),
-        in_specs=[hbm],
-        out_specs=hbm,
-        scratch_shapes=[dma((3,))],
-    )(result)
+    return result.reshape(frames.shape)
 
 
 def solution(mesh):

time: 167 us -> 131 us (0.78)
  Pallas kernels: 165 us -> 125 us
  local copies, waits for them, and re-layouts: 0 us -> 4.5 us
    pallas_call x1 -> x0, Pallas kernels: 54.7 us -> none  [body(): pl.pallas_call(write_out, out_shape=jax.ShapeDtypeStruct(frames.shape, F3...]
    pallas_call x1, Pallas kernels: 111 us -> 125 us  [body(): pl.pallas_call(functools.partial(kernel, depth, cuts), out_shape=jax.Shap...]
    reshape x0 -> x1, local copies, waits for them, and re-layouts: none -> 4.5 us  [body(): return result.reshape(frames.shape)]
where the time goes in v4:
time: 131 us
  Pallas kernels  125 us (95%)
  local copies, waits for them, and re-layouts  4.5 us (3%)
    pallas_call x1, Pallas kernels, body(): pl.pallas_call(functools.partial(kernel, depth, cuts), out_shape=jax.Shap...  125 us
    reshape x1, local copies, waits for them, and re-layouts, body(): return result.reshape(frames.shape)  4.5 us

profile of v4, /device:TPU:0, one launch (start us, length us, event | category | flops | bytes accessed | tf_op | source)
XLA Modules:
  0.0 130.5 jit_solution(12329346315416154758)
XLA Ops:
  0.7 0.1 fusion
  0.7 0.6 pad_maximum_fusion.feats_ref
  1.3 124.7 %shard_map.100 = f32[384,1152]{1,0:T(8,128)} custom-call(f32[1,256]{1,0:T(1,128)} %pad_maximum_fusion.feats_ref, f32[3,1152]{1,0:T(4,128)} %table_s.1, f32[3,1152]{1,0:T(4,128)} %table_t.1, bf16[384,1152]{1,0:T(8,128)(2,1)} %bitcast.8, bf16[256,1152]{1,0:T(8,128)(2,1)} %embed_hbm.1, bf16[144,3456]{1,0:T(8,128)(2,1)} %block_hbm.1, ...), custom_call_target="tpu_custom_call" | custom-call | tf_op jit(solution)/shard_map/pallas_call | solution.py:564
  126.0 4.5 %copy.11 = f32[384,1,1152]{2,1,0:T(1,128)} copy(f32[384,1,1152]{2,0,1:T(8,128)} %bitcast.5) | data formatting | bytes 3538944 | tf_op jit(solution)/shard_map/reshape | solution.py:618

commit v5 on v3

--- a/solution.py
+++ b/solution.py
@@ -510,20 +510,6 @@
         dma((depth,)),
         dma((depth,)),
     ]
-
-
-def write_out(src, dst, sem):
-    rows = src.shape[0] // 3
-    copies = [
-        pltpu.make_async_copy(
-            src.at[pl.ds(i * rows, rows)], dst.at[pl.ds(i * rows, rows), 0, :], sem.at[i]
-        )
-        for i in range(3)
-    ]
-    for copy in copies:
-        copy.start()
-    for copy in copies:
-        copy.wait()
 
 
 def body(
@@ -603,13 +589,7 @@
         jnp.transpose(temporal_qkv, (1, 2, 0)),
         temporal_out,
     )
-    return pl.pallas_call(
-        write_out,
-        out_shape=jax.ShapeDtypeStruct(frames.shape, F32),
-        in_specs=[hbm],
-        out_specs=hbm,
-        scratch_shapes=[dma((3,))],
-    )(result)
+    return result.reshape(frames.shape)
 
 
 def solution(mesh):

time: 167 us -> 117 us (0.70)
  Pallas kernels: 165 us -> 111 us
  local copies, waits for them, and re-layouts: 0 us -> 4.5 us
    pallas_call x1 -> x0, Pallas kernels: 54.7 us -> none  [body(): pl.pallas_call(write_out, out_shape=jax.ShapeDtypeStruct(frames.shape, F3...]
    reshape x0 -> x1, local copies, waits for them, and re-layouts: none -> 4.5 us  [body(): return result.reshape(frames.shape)]
where the time goes in v5:
time: 117 us
  Pallas kernels  111 us (95%)
  local copies, waits for them, and re-layouts  4.5 us (4%)
    pallas_call x1, Pallas kernels, body(): pl.pallas_call(functools.partial(kernel, depth, cuts), out_shape=jax.Shap...  111 us
    reshape x1, local copies, waits for them, and re-layouts, body(): return result.reshape(frames.shape)  4.5 us

profile of v5, /device:TPU:0, one launch (start us, length us, event | category | flops | bytes accessed | tf_op | source)
XLA Modules:
  0.0 116.5 jit_solution(18361186246622073275)
XLA Ops:
  0.7 0.1 fusion
  0.7 0.6 pad_maximum_fusion.feats_ref
  1.3 110.8 %shard_map.100 = f32[384,1152]{1,0:T(8,128)} custom-call(f32[1,256]{1,0:T(1,128)} %pad_maximum_fusion.feats_ref, f32[3,1152]{1,0:T(4,128)} %table_s.1, f32[3,1152]{1,0:T(4,128)} %table_t.1, bf16[384,1152]{1,0:T(8,128)(2,1)} %bitcast.8, bf16[256,1152]{1,0:T(8,128)(2,1)} %embed_hbm.1, bf16[144,3456]{1,0:T(8,128)(2,1)} %block_hbm.1, ...), custom_call_target="tpu_custom_call" | custom-call | tf_op jit(solution)/shard_map/pallas_call | solution.py:540
  112.0 4.5 %copy.11 = f32[384,1,1152]{2,1,0:T(1,128)} copy(f32[384,1,1152]{2,0,1:T(8,128)} %bitcast.5) | data formatting | bytes 3538944 | tf_op jit(solution)/shard_map/reshape | solution.py:592
